TPU v7x, 128 devices: a whole 4x4x4 slice. The times are simulated.
128 devices in a mesh: span: 16 (over y, z), wall: 8 (over x, core).
Axes of the slice: x: 4, y: 4, z: 4, core: 2. Of those that a mesh axis runs over, the one named last changes fastest.
Arguments:
- stress: float32 [2, 32, 1024, 2048], P(None, None, 'wall', 'span'), may hold values from -8 to 8
Outputs:
- pressure: float32 [2, 32, 1024, 2048], P(None, None, 'wall', 'span')
All inputs are finite; a program needn't handle non-finite values.
Results may differ from a plain program's by a relative error of at most 0.00035.
Values sent between devices are 32-bit elements; how exact they have to be, the bound alone decides.
A program may use at most 128 MiB of HBM per device.

v0:
```python
import math
import jax
import jax.numpy as jnp
from jax import lax
from jax.sharding import PartitionSpec as P

stretch_rate = 2.0
span_rate = 2.0 / 3.0
stream_rate = 0.25


def shifted(array, axis, by):
    peers = lax.axis_size(axis)
    pairs = [(i, i + by) for i in range(peers) if 0 <= i + by < peers]
    return lax.ppermute(array, axis, pairs)


def wall_coefficients(count):
    node_index = jnp.arange(count + 1, dtype=jnp.int32)
    xi_left = (2 * node_index - count - 1).astype(jnp.float32) / (count + 1)
    xi_right = (2 * node_index - count + 1).astype(jnp.float32) / (count + 1)
    spacing = jnp.sinh(2.0 * stretch_rate / (count + 1)) / (
        jnp.tanh(stretch_rate)
        * jnp.cosh(stretch_rate * xi_left)
        * jnp.cosh(stretch_rate * xi_right)
    )
    gap_before = spacing[:-1]
    gap_after = spacing[1:]
    lower_band = gap_after / (gap_before + gap_after)
    upper_band = gap_before / (gap_before + gap_after)
    weight = 0.5 * gap_before * gap_after
    return (lower_band, upper_band, weight)


def wave_squares(length, block_width, mode_ids):
    mode_index = jnp.arange(block_width, dtype=jnp.int32)
    signed = jnp.where(mode_index >= length // 2, mode_index - length, mode_index)
    span_wave = signed.astype(jnp.float32) * span_rate
    stream_wave = mode_ids.astype(jnp.float32) * stream_rate
    wave_sq = stream_wave[:, None] ** 2 + span_wave[None, :] ** 2
    return (wave_sq, span_wave**2)


def thomas(lower_band, upper_band, weight, wave_sq, rows):

    def forward(state, row_data):
        ratio_prev, value_prev = state
        low_entry, upp_entry, wei_entry, row_now = row_data
        pivot_value = 1.0 + wave_sq * wei_entry + low_entry * ratio_prev
        ratio_new = -upp_entry / pivot_value
        value_new = (row_now + low_entry * value_prev) / pivot_value
        return ((ratio_new, value_new), (ratio_new, value_new))

    start_state = (jnp.zeros(rows.shape[2:], jnp.float32), jnp.zeros(rows.shape[1:], jnp.float32))
    final_state, sweeps = lax.scan(
        forward, start_state, (lower_band, upper_band, weight, rows), unroll=4
    )

    def backward(after_value, row_data):
        ratio_now, value_now = row_data
        value_here = value_now - ratio_now[None] * after_value
        return (value_here, value_here)

    final_value, solution = lax.scan(
        backward, jnp.zeros(rows.shape[1:], jnp.float32), sweeps, reverse=True, unroll=4
    )
    return solution


def factor_pair(length):
    factor = 1
    for divisor in range(1, math.isqrt(length) + 1):
        if length % divisor == 0:
            factor = divisor
    return (factor, length // factor)


def phase_table(row_count, col_count, length, sign):
    row_ids = jnp.arange(row_count, dtype=jnp.int32)[:, None]
    col_ids = jnp.arange(col_count, dtype=jnp.int32)[None, :]
    angle_table = (row_ids * col_ids % length).astype(jnp.float32) * (2.0 * math.pi / length)
    return (jnp.cos(angle_table), sign * jnp.sin(angle_table))


def factored_dft(real_in, imag_in, sign):
    length = real_in.shape[-1]
    inner_len, outer_len = factor_pair(length)
    leading = real_in.shape[:-1]
    real_grid = real_in.reshape(leading + (outer_len, inner_len))
    imag_grid = imag_in.reshape(leading + (outer_len, inner_len))
    cos_outer, sin_outer = phase_table(outer_len, outer_len, outer_len, sign)
    high = lax.Precision.HIGHEST
    first_real = jnp.einsum("...za,zm->...ma", real_grid, cos_outer, precision=high) - jnp.einsum(
        "...za,zm->...ma", imag_grid, sin_outer, precision=high
    )
    first_imag = jnp.einsum("...za,zm->...ma", real_grid, sin_outer, precision=high) + jnp.einsum(
        "...za,zm->...ma", imag_grid, cos_outer, precision=high
    )
    cos_twid, sin_twid = phase_table(outer_len, inner_len, length, sign)
    twid_real = first_real * cos_twid - first_imag * sin_twid
    twid_imag = first_real * sin_twid + first_imag * cos_twid
    cos_inner, sin_inner = phase_table(inner_len, inner_len, inner_len, sign)
    last_real = jnp.einsum("...ma,an->...nm", twid_real, cos_inner, precision=high) - jnp.einsum(
        "...ma,an->...nm", twid_imag, sin_inner, precision=high
    )
    last_imag = jnp.einsum("...ma,an->...nm", twid_real, sin_inner, precision=high) + jnp.einsum(
        "...ma,an->...nm", twid_imag, cos_inner, precision=high
    )
    return (last_real.reshape(leading + (length,)), last_imag.reshape(leading + (length,)))


def body(stress):
    mode_count = stress.shape[1]
    rows_dev = stress.shape[2]
    span_count = lax.axis_size("span")
    wall_count = lax.axis_size("wall")
    mode_dev = mode_count // span_count
    length = stress.shape[3] * span_count
    wall_cells = rows_dev * wall_count
    wall_at = lax.axis_index("wall")
    span_at = lax.axis_index("span")
    lower_all, upper_all, weight_all = wall_coefficients(wall_cells)
    row_start = wall_at * rows_dev
    lower_band = lax.dynamic_slice_in_dim(lower_all, row_start, rows_dev)
    upper_band = lax.dynamic_slice_in_dim(upper_all, row_start, rows_dev)
    weight = lax.dynamic_slice_in_dim(weight_all, row_start, rows_dev)
    mode_ids = span_at * mode_dev + jnp.arange(mode_dev, dtype=jnp.int32)
    wave_sq, span_sq = wave_squares(length, length, mode_ids)
    received = lax.all_to_all(stress, "span", split_axis=1, concat_axis=3, tiled=True)
    real_part, imag_part = factored_dft(received[0], received[1], -1.0)
    stacked = jnp.stack([real_part, imag_part], axis=0)
    spectral = jnp.transpose(stacked, (2, 0, 1, 3))
    source = spectral * weight[:, None, None, None] * span_sq[None, None, None, :]
    inner = rows_dev - 1
    row_index = jnp.arange(inner, dtype=jnp.int32)
    alpha_col = jnp.where(row_index == 0, lower_band[0], 0.0)
    beta_col = jnp.where(row_index == inner - 1, upper_band[inner - 1], 0.0)
    upper_inner = jnp.where(row_index == inner - 1, 0.0, upper_band[:inner])
    ones_block = jnp.ones((inner, 1, mode_dev, length), jnp.float32)
    extended = jnp.concatenate(
        [
            source[:inner],
            ones_block * alpha_col[:, None, None, None],
            ones_block * beta_col[:, None, None, None],
        ],
        axis=1,
    )
    local_part = thomas(lower_band[:inner], upper_inner, weight[:inner], wave_sq, extended)
    next_rows = shifted(local_part[0], "wall", -1)
    last_rows = local_part[inner - 1]
    sep_lower = lower_band[inner]
    sep_upper = upper_band[inner]
    sep_diag = 1.0 + wave_sq * weight[inner]
    coef_a = -sep_lower * last_rows[2]
    coef_b = sep_diag - sep_lower * last_rows[3] - sep_upper * next_rows[2]
    coef_c = -sep_upper * next_rows[3]
    coef_r = source[inner] + sep_lower * last_rows[0:2] + sep_upper * next_rows[0:2]
    levels = wall_count.bit_length() - 1
    for level in range(levels):
        stride = 1 << level
        packed = jnp.concatenate([coef_a[None], coef_b[None], coef_c[None], coef_r], axis=0)
        below_rows = shifted(packed, "wall", stride)
        above_rows = shifted(packed, "wall", -stride)
        below_pivot = below_rows[1] + (wall_at < stride).astype(jnp.float32)
        above_pivot = above_rows[1] + (wall_at + stride >= wall_count).astype(jnp.float32)
        left_factor = coef_a / below_pivot
        right_factor = coef_c / above_pivot
        new_a = -left_factor * below_rows[0]
        new_c = -right_factor * above_rows[2]
        new_b = coef_b - left_factor * below_rows[2] - right_factor * above_rows[0]
        new_r = coef_r - left_factor[None] * below_rows[3:5] - right_factor[None] * above_rows[3:5]
        coef_a, coef_b, coef_c, coef_r = (new_a, new_b, new_c, new_r)
    value_here = coef_r / coef_b[None]
    value_prev = shifted(value_here, "wall", 1)
    inner_rows = (
        local_part[:, 0:2]
        + local_part[:, 2:3] * value_prev[None]
        + local_part[:, 3:4] * value_here[None]
    )
    pressure_rows = jnp.concatenate([inner_rows, value_here[None]], axis=0)
    back_real, back_imag = factored_dft(pressure_rows[:, 0], pressure_rows[:, 1], 1.0)
    stacked = jnp.stack([back_real / length, back_imag / length], axis=0)
    physical = jnp.transpose(stacked, (0, 2, 1, 3))
    return lax.all_to_all(physical, "span", split_axis=3, concat_axis=1, tiled=True)


def solution(mesh):
    placed = (P(None, None, "wall", "span"),)
    return jax.shard_map(
        body, mesh=mesh, in_specs=placed, out_specs=P(None, None, "wall", "span"), check_vma=False
    )
```

profile of v0, /device:TPU:1, one launch (start us, length us, event | category | flops | bytes accessed | tf_op | source)
XLA Modules:
  0.0 899.3 jit_solution(15733420314305276271)
XLA Ops:
  0.0 4.7 copy.196
  4.7 8.6 all-to-all-start
  20.8 54.0 %all-to-all-done = f32[2,32,128,128]{3,2,0,1:T(8,128)} async-done(((f32[2,32,128,128]{3,2,0,1:T(8,128)}), f32[2,32,128,128]{3,2,0,1:T(8,128)}, u32[]{:S(2)}, u32[]{:S(2)}) %all-to-all-start) | async-done | bytes 4194336 | tf_op jit(solution)/shard_map/all_to_all | solution.py:129
  81.6 4.5 fusion.56
  86.0 4.4 fusion.58
  92.6 4.9 fusion.64
  97.5 4.1 subtract_bitcast_fusion.2
  119.6 13.7 %slice_reduce_fusion.2 = (f32[4,2,2048]{2,1,0:T(2,128)S(1)}, f32[4,2,2048]{2,1,0:T(2,128)S(1)}, f32[4,2,2048]{2,1,0:T(2,128)S(1)}) fusion(f32[127,4,2,2048]{0,3,2,1:T(8,128)S(1)} %pad_maximum_fusion), kind=kLoop, calls=%fused_computation.57 | loop fusion | bytes 393216 | tf_op jit(solution)/shard_map/slice | solution.py:55
  133.2 13.4 %copy.210 = f32[124,4,2,2048]{3,2,1,0:T(2,128)} copy(f32[124,4,2,2048]{0,3,2,1:T(8,128)} %bitcast.361) | data formatting | bytes 16252928 | tf_op jit(solution)/shard_map/slice | solution.py:55
  146.6 7.3 broadcast.408.clone
  153.9 447.0 %while.34 = (s32[]{:T(128)}, f32[2,2048]{1,0:T(2,128)S(1)}, f32[4,2,2048]{2,1,0:T(2,128)S(1)}, f32[31,4,2,2048]{3,2,1,0:T(2,128)}, f32[31,4,4,2,2048]{4,3,2,1,0:...) while((s32[]{:T(128)}, f32[2,2048]{1,0:T(2,128)S(1)}, ...), condition=%wide.region_1.2_spmd.clone, body=%wide.region_0.1_spmd.clone.sunk | while | flops 548874 | bytes 1466900 | solution.py:55
  158.3 4.9 broadcast_divide_fusion.12
  172.8 4.9 broadcast_divide_fusion.12
  187.2 4.9 broadcast_divide_fusion.12
  192.1 3.5 fusion.300
  201.6 4.9 broadcast_divide_fusion.12
  206.5 3.5 fusion.300
  216.0 4.9 broadcast_divide_fusion.12
  230.4 4.9 broadcast_divide_fusion.12
  235.4 3.5 fusion.300
  244.8 4.9 broadcast_divide_fusion.12
  259.2 4.9 broadcast_divide_fusion.12
  273.6 4.9 broadcast_divide_fusion.12
  288.1 4.9 broadcast_divide_fusion.12
  302.5 4.9 broadcast_divide_fusion.12
  316.9 4.9 broadcast_divide_fusion.12
  331.3 4.9 broadcast_divide_fusion.12
  345.7 4.9 broadcast_divide_fusion.12
  360.2 4.9 broadcast_divide_fusion.12
  374.6 4.9 broadcast_divide_fusion.12
  389.0 4.9 broadcast_divide_fusion.12
  403.4 4.9 broadcast_divide_fusion.12
  417.9 4.9 broadcast_divide_fusion.12
  432.3 4.9 broadcast_divide_fusion.12
  446.7 4.9 broadcast_divide_fusion.12
  461.1 4.9 broadcast_divide_fusion.12
  475.5 4.9 broadcast_divide_fusion.12
  489.9 4.9 broadcast_divide_fusion.12
  504.3 4.9 broadcast_divide_fusion.12
  518.8 4.9 broadcast_divide_fusion.12
  533.2 4.9 broadcast_divide_fusion.12
  547.6 4.9 broadcast_divide_fusion.12
  562.1 4.9 broadcast_divide_fusion.12
  576.5 4.9 broadcast_divide_fusion.12
  590.9 4.9 broadcast_divide_fusion.12
  601.6 3.7 divide_bitcast_fusion.1
  609.7 8.3 pad_maximum_fusion.2
  618.1 7.3 broadcast.408
  625.4 86.7 %while.35 = (s32[]{:T(128)}, f32[4,2,2048]{2,1,0:T(2,128)S(1)}, f32[31,4,4,2,2048]{4,3,2,1,0:T(2,128)}, f32[31,4,4,2,2048]{4,3,2,1,0:T(2,128)}, f32[31,4,2,2048]...) while((s32[]{:T(128)}, f32[4,2,2048]{2,1,0:T(2,128)S(1)}, ...), condition=%wide.region_3.4_spmd.clone, body=%wide.region_2.3_spmd.clone.sunk | while | flops 376839 | bytes 1458395 | solution.py:64
  715.5 4.3 collective-permute-start
  722.4 6.3 fusion.27
  745.7 4.2 collective-permute-done.4
  751.3 5.5 collective-permute-start.5
  756.9 7.9 pad_maximum_fusion.1
  764.8 4.1 collective-permute-start.7
  771.9 6.4 fusion.30
  778.3 3.7 fusion.31
  784.8 4.5 fusion.40
  789.2 4.4 fusion.42
  796.8 4.9 fusion.74
  801.7 4.1 subtract_bitcast_fusion
  821.2 10.5 %copy.227 = f32[2,2,128,2048]{2,1,0,3:T(2,128)S(1)} copy(f32[2,2,128,2048]{2,3,1,0:T(8,128)S(1)} %maximum_bitcast_fusion.3) | data formatting | bytes 8388608 | tf_op jit(solution)/shard_map/transpose | solution.py:183
  831.7 59.8 %all_to_all.33 = f32[2,2,128,2048]{2,1,0,3:T(2,128)S(1)} all-to-all(f32[2,2,128,2048]{2,1,0,3:T(2,128)S(1)} %copy.227), channel_id=1, replica_groups=mesh['span'=16,'wall'=8] {'span'}, dimensions={3} | all-to-all | bytes 8388608 | tf_op jit(solution)/shard_map/all_to_all | solution.py:184
  893.7 5.3 copy.229
  (465 shorter events, 379.7 us)
Async XLA Ops:
  4.7 70.2 %all-to-all-start = ((f32[2,32,128,128]{3,2,0,1:T(8,128)}), f32[2,32,128,128]{3,2,0,1:T(8,128)}, u32[]{:S(2)}, u32[]{:S(2)}) async-start(f32[2,32,128,128]{3,2,0,1:T(8,128)} %copy.196), calls=%async_computation | async-start | bytes 8388608 | tf_op jit(solution)/shard_map/all_to_all | solution.py:129
  92.6 4.9 copy-start.2
  117.0 2.0 copy-start.1
  119.6 13.7 %copy-start = (f32[127,4,2,2048]{0,3,2,1:T(8,128)}, f32[127,4,2,2048]{0,3,2,1:T(8,128)S(1)}, u32[]{:S(2)}) copy-start(f32[127,4,2,2048]{0,3,2,1:T(8,128)S(1)} %pad_maximum_fusion) | copy-start | bytes 24969220
  715.5 13.3 %collective-permute-start = (f32[4,2,2048]{2,1,0:T(2,128)S(1)}, f32[4,2,2048]{2,1,0:T(2,128)S(1)}, u32[]{:S(2)}, u32[]{:S(2)}) collective-permute-start(f32[4,2,2048]{2,1,0:T(2,128)S(1)} %fusion.86), channel_id=1, source_target_pairs={{1,0},{2,1},{3,2},{4,3},{5,4},{6,5},{7,6},{9,8},{10,9},{11,10},{12... | collective-permute-start | bytes 196616 | tf_op jit(solution)/shard_map/ppermute | solution.py:15
  732.1 5.0 collective-permute-start.1
  735.1 5.8 collective-permute-start.2
  741.0 4.7 collective-permute-start.3
  744.2 5.7 collective-permute-start.4
  750.0 14.7 %collective-permute-start.6 = (f32[5,2,2048]{2,1,0:T(2,128)S(1)}, f32[5,2,2048]{2,1,0:T(2,128)S(1)}, u32[]{:S(2)}, u32[]{:S(2)}) collective-permute-start(f32[5,2,2048]{2,1,0:T(2,128)S(1)} %pad_maximum_fusion.11), channel_id=1, source_target_pairs={{4,0},{5,1},{6,2},{7,3},{12,8},{13,9},{14,10},{15,11},{20,16},{21,... | collective-permute-start | bytes 245768 | tf_op jit(solution)/shard_map/ppermute | solution.py:15
  751.3 13.4 %collective-permute-start.5 = (f32[5,2,2048]{2,1,0:T(2,128)S(1)}, f32[5,2,2048]{2,1,0:T(2,128)S(1)}, u32[]{:S(2)}, u32[]{:S(2)}) collective-permute-start(f32[5,2,2048]{2,1,0:T(2,128)S(1)} %pad_maximum_fusion.11), channel_id=1, source_target_pairs={{0,4},{1,5},{2,6},{3,7},{8,12},{9,13},{10,14},{11,15},{16,20},{17,... | collective-permute-start | bytes 245768 | tf_op jit(solution)/shard_map/ppermute | solution.py:15
  756.8 12.1 %slice-start = ((s8[8126464]{0:T(1024)(128)(4,1)}), s8[4194304]{0:T(1024)(128)(4,1)S(1)}, s32[]{:S(2)}) async-start(s8[8126464]{0:T(1024)(128)(4,1)} %bitcast.367), calls=%async_computation.2 | async-start | bytes 8388608
  756.9 12.1 %slice-start.1 = ((s8[8126464]{0:T(1024)(128)(4,1)}), s8[3932160]{0:T(1024)(128)(4,1)S(1)}, s32[]{:S(2)}) async-start(s8[8126464]{0:T(1024)(128)(4,1)} %bitcast.367), calls=%async_computation.3 | async-start | bytes 7864320
  764.8 7.1 collective-permute-start.7
  796.8 4.9 copy-start.3
where the time goes:
time: 916 us; the launch traced here: 899 us
  other arithmetic  449 us (49%)
  local copies, waits for them, and re-layouts  154 us (17%)
  loops' own time  77 us (8%)
  waiting for transfers between devices  61.4 us (7%)
  matrix products  60.8 us (7%)
  blocking collectives  59.8 us (7%)
  starting transfers between devices  33.2 us (4%)
    div x31, other arithmetic, forward(): ratio_new = -upp_entry / pivot_value  153 us
    div x31, other arithmetic, forward(): value_new = (row_now + low_entry * value_prev) / pivot_value  109 us
    slice x96, local copies, waits for them, and re-layouts, thomas(): lax.scan(forward, start_state, (lower_band, upper_band, weight, rows), un...  88.1 us
    another operation x1, loops' own time, thomas(): lax.scan(forward, start_state, (lower_band, upper_band, weight, rows), un...  76.8 us
    dynamic_update_slice x93, other arithmetic, thomas(): lax.scan(forward, start_state, (lower_band, upper_band, weight, rows), un...  72.8 us
    all_to_all x1, blocking collectives, body(): lax.all_to_all(physical, 'span', split_axis=3, concat_axis=1, tiled=True)  59.8 us
    all_to_all x1, waiting for transfers between devices, body(): lax.all_to_all(stress, 'span', split_axis=1, concat_axis=3, tiled=True)  54 us
    broadcast_in_dim x32, other arithmetic, thomas(): lax.scan(backward, jnp.zeros(rows.shape[1:], jnp.float32), sweeps, revers...  32.1 us
  transfers between devices with their start and end apart: 9, of which 4 were waited for; matrix products, arithmetic and copies ran while one was open for 3% of the time, Pallas kernels for 0%

commit v1 on v0

--- a/solution.py
+++ b/solution.py
@@ -7,6 +7,29 @@
 stretch_rate = 2.0
 span_rate = 2.0 / 3.0
 stream_rate = 0.25
+
+
+def cut_along(array, dim, length):
+    shape = array.shape
+    blocks = array.reshape(*shape[:dim], length, shape[dim] // length, *shape[dim + 1 :])
+    return jnp.moveaxis(blocks, dim, 0)
+
+
+def in_order(pieces, dim):
+    dims = list(pieces.shape[1:])
+    dims[dim] *= pieces.shape[0]
+    return jnp.moveaxis(pieces, 0, dim).reshape(dims)
+
+
+def rotated_exchange(array, axis, split_dim, concat_dim):
+    devices, index = (lax.axis_size(axis), lax.axis_index(axis))
+    tiles = cut_along(array, split_dim, devices)
+    outs = [tiles[index]]
+    for step in range(1, devices):
+        sent = tiles[(index + step) % devices]
+        outs.append(lax.ppermute(sent, axis, [(i, (i + step) % devices) for i in range(devices)]))
+    tiles = jnp.stack(outs)[(index - jnp.arange(devices)) % devices]
+    return in_order(tiles, concat_dim)
 
 
 def shifted(array, axis, by):
@@ -126,7 +149,7 @@
     weight = lax.dynamic_slice_in_dim(weight_all, row_start, rows_dev)
     mode_ids = span_at * mode_dev + jnp.arange(mode_dev, dtype=jnp.int32)
     wave_sq, span_sq = wave_squares(length, length, mode_ids)
-    received = lax.all_to_all(stress, "span", split_axis=1, concat_axis=3, tiled=True)
+    received = rotated_exchange(stress, "span", 1, 3)
     real_part, imag_part = factored_dft(received[0], received[1], -1.0)
     stacked = jnp.stack([real_part, imag_part], axis=0)
     spectral = jnp.transpose(stacked, (2, 0, 1, 3))

time: 916 us -> 967 us (1.056)
  starting transfers between devices: 33.2 us -> 69.6 us
  local copies, waits for them, and re-layouts: 154 us -> 176 us
  waiting for transfers between devices: 61.4 us -> 51.1 us
    all_to_all x1 -> x0, waiting for transfers between devices: 54 us -> none  [body(): lax.all_to_all(stress, 'span', split_axis=1, concat_axis=3, tiled=True)]
    ppermute x0 -> x15, waiting for transfers between devices: none -> 43.7 us  [rotated_exchange(): lax.ppermute(sent, axis, [(i, (i + step) % devices) for i in range(device...]
    ppermute x0 -> x15, starting transfers between devices: none -> 28.4 us  [rotated_exchange(): lax.ppermute(sent, axis, [(i, (i + step) % devices) for i in range(device...]
    ppermute x8, starting transfers between devices: 24.5 us -> 41.3 us  [shifted(): return lax.ppermute(array, axis, pairs)]
    unnamed x14 -> x28, local copies, waits for them, and re-layouts: 9.09 us -> 20 us
  transfers between devices with their start and end apart: 9 -> 23, of which waited for: 4 -> 12; matrix products, arithmetic and copies ran while one was open for 3% -> 4% of each run, Pallas kernels for 0% -> 0%
where the time goes in v1:
time: 967 us; the launch traced here: 951 us
  other arithmetic  454 us (47%)
  local copies, waits for them, and re-layouts  176 us (18%)
  loops' own time  77.4 us (8%)
  starting transfers between devices  69.6 us (7%)
  matrix products  60.8 us (6%)
  blocking collectives  57.4 us (6%)
  waiting for transfers between devices  51.1 us (5%)
    div x31, other arithmetic, forward(): ratio_new = -upp_entry / pivot_value  158 us
    div x31, other arithmetic, forward(): value_new = (row_now + low_entry * value_prev) / pivot_value  110 us
    slice x96, local copies, waits for them, and re-layouts, thomas(): lax.scan(forward, start_state, (lower_band, upper_band, weight, rows), un...  89 us
    another operation x1, loops' own time, thomas(): lax.scan(forward, start_state, (lower_band, upper_band, weight, rows), un...  77.2 us
    dynamic_update_slice x93, other arithmetic, thomas(): lax.scan(forward, start_state, (lower_band, upper_band, weight, rows), un...  72.9 us
    all_to_all x1, blocking collectives, body(): lax.all_to_all(physical, 'span', split_axis=3, concat_axis=1, tiled=True)  57.4 us
    ppermute x15, waiting for transfers between devices, rotated_exchange(): lax.ppermute(sent, axis, [(i, (i + step) % devices) for i in range(device...  43.7 us
    ppermute x8, starting transfers between devices, shifted(): return lax.ppermute(array, axis, pairs)  41.3 us
  transfers between devices with their start and end apart: 23, of which 12 were waited for; matrix products, arithmetic and copies ran while one was open for 4% of the time, Pallas kernels for 0%

profile of v1, /device:TPU:1, one launch (start us, length us, event | category | flops | bytes accessed | tf_op | source)
XLA Modules:
  0.0 950.8 jit_solution(3416178161019128784)
XLA Ops:
  3.2 7.0 collective-permute-start.14
  22.9 16.3 %collective-permute-done = f32[2,2,128,128]{3,2,1,0:T(8,128)} collective-permute-done((f32[2,2,128,128]{3,2,1,0:T(8,128)}, f32[2,2,128,128]{3,2,1,0:T(8,128)}, u32[]{:S(2)}, u32[]{:S(2)}) %collective-permute-start) | collective-permute-done | bytes 262176 | tf_op jit(solution)/shard_map/ppermute | solution.py:30
  52.6 4.2 collective-permute-done.4
  59.7 6.4 collective-permute-done.5
  74.5 4.3 collective-permute-start.9
  79.6 5.3 collective-permute-start.10
  89.0 5.6 collective-permute-done.11
  100.3 5.0 gather_fusion
  105.2 4.8 fusion.277
  111.9 4.4 fusion.56
  116.4 4.4 fusion.58
  123.2 4.9 fusion.64
  150.1 13.5 %slice_reduce_fusion.2 = (f32[4,2,2048]{2,1,0:T(2,128)S(1)}, f32[4,2,2048]{2,1,0:T(2,128)S(1)}, f32[4,2,2048]{2,1,0:T(2,128)S(1)}) fusion(f32[127,4,2,2048]{0,3,2,1:T(8,128)S(1)} %pad_maximum_fusion), kind=kLoop, calls=%fused_computation.58 | loop fusion | bytes 393216 | tf_op jit(solution)/shard_map/slice | solution.py:78
  163.6 13.3 %copy.304 = f32[124,4,2,2048]{3,2,1,0:T(2,128)} copy(f32[124,4,2,2048]{0,3,2,1:T(8,128)} %bitcast.456) | data formatting | bytes 16252928 | tf_op jit(solution)/shard_map/slice | solution.py:78
  176.9 7.3 broadcast.486.clone
  184.2 453.3 %while.34 = (s32[]{:T(128)}, f32[2,2048]{1,0:T(2,128)S(1)}, f32[4,2,2048]{2,1,0:T(2,128)S(1)}, f32[31,4,2,2048]{3,2,1,0:T(2,128)}, f32[31,4,4,2,2048]{4,3,2,1,0:...) while((s32[]{:T(128)}, f32[2,2048]{1,0:T(2,128)S(1)}, ...), condition=%wide.region_1.2_spmd.clone, body=%wide.region_0.1_spmd.clone.sunk | while | flops 548874 | bytes 1466900 | solution.py:78
  188.7 5.1 broadcast_divide_fusion.12
  203.3 5.1 broadcast_divide_fusion.12
  217.9 5.1 broadcast_divide_fusion.12
  232.5 5.1 broadcast_divide_fusion.12
  247.2 5.1 broadcast_divide_fusion.12
  261.8 5.1 broadcast_divide_fusion.12
  276.4 5.1 broadcast_divide_fusion.12
  291.0 5.1 broadcast_divide_fusion.12
  305.7 5.1 broadcast_divide_fusion.12
  320.3 5.1 broadcast_divide_fusion.12
  334.9 5.1 broadcast_divide_fusion.12
  349.5 5.1 broadcast_divide_fusion.12
  364.2 5.1 broadcast_divide_fusion.12
  378.8 5.1 broadcast_divide_fusion.12
  393.4 5.1 broadcast_divide_fusion.12
  408.0 5.1 broadcast_divide_fusion.12
  422.6 5.1 broadcast_divide_fusion.12
  437.3 5.1 broadcast_divide_fusion.12
  451.9 5.1 broadcast_divide_fusion.12
  466.5 5.1 broadcast_divide_fusion.12
  481.1 5.1 broadcast_divide_fusion.12
  495.8 5.1 broadcast_divide_fusion.12
  510.4 5.1 broadcast_divide_fusion.12
  525.0 5.1 broadcast_divide_fusion.12
  539.6 5.1 broadcast_divide_fusion.12
  554.3 5.1 broadcast_divide_fusion.12
  568.9 5.1 broadcast_divide_fusion.12
  583.5 5.1 broadcast_divide_fusion.12
  598.1 5.1 broadcast_divide_fusion.12
  612.7 5.1 broadcast_divide_fusion.12
  627.4 5.1 broadcast_divide_fusion.12
  646.5 8.6 pad_maximum_fusion.2
  655.1 7.3 broadcast.486
  662.4 86.7 %while.35 = (s32[]{:T(128)}, f32[4,2,2048]{2,1,0:T(2,128)S(1)}, f32[31,4,4,2,2048]{4,3,2,1,0:T(2,128)}, f32[31,4,4,2,2048]{4,3,2,1,0:T(2,128)}, f32[31,4,2,2048]...) while((s32[]{:T(128)}, f32[4,2,2048]{2,1,0:T(2,128)S(1)}, ...), condition=%wide.region_3.4_spmd.clone, body=%wide.region_2.3_spmd.clone.sunk | while | flops 376839 | bytes 1458395 | solution.py:87
  752.5 21.0 %collective-permute-start.15 = (f32[4,2,2048]{2,1,0:T(2,128)S(1)}, f32[4,2,2048]{2,1,0:T(2,128)S(1)}, u32[]{:S(2)}, u32[]{:S(2)}) collective-permute-start(f32[4,2,2048]{2,1,0:T(2,128)S(1)} %fusion.86), channel_id=1, source_target_pairs={{1,0},{2,1},{3,2},{4,3},{5,4},{6,5},{7,6},{9,8},{10,9},{11,10},{12... | collective-permute-start | bytes 196616 | tf_op jit(solution)/shard_map/ppermute | solution.py:38
  776.2 6.4 fusion.27
  799.6 4.2 collective-permute-done.19
  805.2 5.5 collective-permute-start.20
  810.7 7.9 pad_maximum_fusion.1
  818.7 4.1 collective-permute-start.22
  825.7 6.4 fusion.30
  838.5 4.4 fusion.40
  843.0 4.4 fusion.42
  850.4 4.9 fusion.74
  855.3 4.1 subtract_bitcast_fusion
  874.8 10.5 %copy.321 = f32[2,2,128,2048]{2,1,0,3:T(2,128)S(1)} copy(f32[2,2,128,2048]{2,3,1,0:T(8,128)S(1)} %maximum_bitcast_fusion.3) | data formatting | bytes 8388608 | tf_op jit(solution)/shard_map/transpose | solution.py:206
  885.3 57.4 %all_to_all.18 = f32[2,2,128,2048]{2,1,0,3:T(2,128)S(1)} all-to-all(f32[2,2,128,2048]{2,1,0,3:T(2,128)S(1)} %copy.321), channel_id=1, replica_groups=mesh['span'=16,'wall'=8] {'span'}, dimensions={3} | all-to-all | bytes 8388608 | tf_op jit(solution)/shard_map/all_to_all | solution.py:207
  945.0 5.3 copy.323
  (511 shorter events, 442.3 us)
Async XLA Ops:
  3.2 95.4 %collective-permute-start.14 = (f32[2,2,128,128]{3,2,1,0:T(8,128)S(1)}, f32[2,2,128,128]{3,2,1,0:T(8,128)}, u32[]{:S(2)}, u32[]{:S(2)}) collective-permute-start(f32[2,2,128,128]{3,2,1,0:T(8,128)S(1)} %get-tuple-element.416), channel_id=1, source_target_pairs={{0,120},{8,0},{16,8},{24,16},{32,24},{40,32},{48,40},{56,48},{64,5... | collective-permute-start | bytes 786440 | tf_op jit(solution)/shard_map/ppermute | solution.py:30
  10.2 86.7 %collective-permute-start.13 = (f32[2,2,128,128]{3,2,1,0:T(8,128)S(1)}, f32[2,2,128,128]{3,2,1,0:T(8,128)}, u32[]{:S(2)}, u32[]{:S(2)}) collective-permute-start(f32[2,2,128,128]{3,2,1,0:T(8,128)S(1)} %get-tuple-element.417), channel_id=1, source_target_pairs={{0,112},{8,120},{16,0},{24,8},{32,16},{40,24},{48,32},{56,40},{64,... | collective-permute-start | bytes 786440 | tf_op jit(solution)/shard_map/ppermute | solution.py:30
  10.2 85.0 %collective-permute-start.12 = (f32[2,2,128,128]{3,2,1,0:T(8,128)S(1)}, f32[2,2,128,128]{3,2,1,0:T(8,128)}, u32[]{:S(2)}, u32[]{:S(2)}) collective-permute-start(f32[2,2,128,128]{3,2,1,0:T(8,128)S(1)} %get-tuple-element.418), channel_id=1, source_target_pairs={{0,104},{8,112},{16,120},{24,0},{32,8},{40,16},{48,24},{56,32},{64... | collective-permute-start | bytes 786440 | tf_op jit(solution)/shard_map/ppermute | solution.py:30
  11.1 31.9 %collective-permute-start.1 = (f32[2,2,128,128]{3,2,1,0:T(8,128)}, f32[2,2,128,128]{3,2,1,0:T(8,128)}, u32[]{:S(2)}, u32[]{:S(2)}) collective-permute-start(f32[2,2,128,128]{3,2,1,0:T(8,128)} %get-tuple-element.429), channel_id=1, source_target_pairs={{0,16},{8,24},{16,32},{24,40},{32,48},{40,56},{48,64},{56,72},{64,... | collective-permute-start | bytes 786440 | tf_op jit(solution)/shard_map/ppermute | solution.py:30
  13.2 26.1 %collective-permute-start = (f32[2,2,128,128]{3,2,1,0:T(8,128)}, f32[2,2,128,128]{3,2,1,0:T(8,128)}, u32[]{:S(2)}, u32[]{:S(2)}) collective-permute-start(f32[2,2,128,128]{3,2,1,0:T(8,128)} %get-tuple-element.430), channel_id=1, source_target_pairs={{0,8},{8,16},{16,24},{24,32},{32,40},{40,48},{48,56},{56,64},{64,7... | collective-permute-start | bytes 786440 | tf_op jit(solution)/shard_map/ppermute | solution.py:30
  39.2 8.0 collective-permute-start.2
  43.0 8.3 collective-permute-start.3
  47.2 9.5 %collective-permute-start.4 = (f32[2,2,128,128]{3,2,1,0:T(8,128)S(1)}, f32[2,2,128,128]{3,2,1,0:T(8,128)S(1)}, u32[]{:S(2)}, u32[]{:S(2)}) collective-permute-start(f32[2,2,128,128]{3,2,1,0:T(8,128)S(1)} %get-tuple-element.426), channel_id=1, source_target_pairs={{0,40},{8,48},{16,56},{24,64},{32,72},{40,80},{48,88},{56,96},{64,... | collective-permute-start | bytes 786440 | tf_op jit(solution)/shard_map/ppermute | solution.py:30
  51.2 14.9 %collective-permute-start.5 = (f32[2,2,128,128]{3,2,1,0:T(8,128)S(1)}, f32[2,2,128,128]{3,2,1,0:T(8,128)S(1)}, u32[]{:S(2)}, u32[]{:S(2)}) collective-permute-start(f32[2,2,128,128]{3,2,1,0:T(8,128)S(1)} %get-tuple-element.425), channel_id=1, source_target_pairs={{0,48},{8,56},{16,64},{24,72},{32,80},{40,88},{48,96},{56,104},{64... | collective-permute-start | bytes 786440 | tf_op jit(solution)/shard_map/ppermute | solution.py:30
  56.8 10.9 %collective-permute-start.6 = (f32[2,2,128,128]{3,2,1,0:T(8,128)S(1)}, f32[2,2,128,128]{3,2,1,0:T(8,128)S(1)}, u32[]{:S(2)}, u32[]{:S(2)}) collective-permute-start(f32[2,2,128,128]{3,2,1,0:T(8,128)S(1)} %get-tuple-element.424), channel_id=1, source_target_pairs={{0,56},{8,64},{16,72},{24,80},{32,88},{40,96},{48,104},{56,112},{6... | collective-permute-start | bytes 786440 | tf_op jit(solution)/shard_map/ppermute | solution.py:30
  66.1 8.4 collective-permute-start.7
  67.7 11.9 %collective-permute-start.8 = (f32[2,2,128,128]{3,2,1,0:T(8,128)S(1)}, f32[2,2,128,128]{3,2,1,0:T(8,128)S(1)}, u32[]{:S(2)}, u32[]{:S(2)}) collective-permute-start(f32[2,2,128,128]{3,2,1,0:T(8,128)S(1)} %get-tuple-element.422), channel_id=1, source_target_pairs={{0,72},{8,80},{16,88},{24,96},{32,104},{40,112},{48,120},{56,0},{6... | collective-permute-start | bytes 786440 | tf_op jit(solution)/shard_map/ppermute | solution.py:30
  74.5 11.1 %collective-permute-start.9 = (f32[2,2,128,128]{3,2,1,0:T(8,128)S(1)}, f32[2,2,128,128]{3,2,1,0:T(8,128)S(1)}, u32[]{:S(2)}, u32[]{:S(2)}) collective-permute-start(f32[2,2,128,128]{3,2,1,0:T(8,128)S(1)} %get-tuple-element.421), channel_id=1, source_target_pairs={{0,80},{8,88},{16,96},{24,104},{32,112},{40,120},{48,0},{56,8},{64... | collective-permute-start | bytes 786440 | tf_op jit(solution)/shard_map/ppermute | solution.py:30
  79.6 8.6 collective-permute-start.10
  85.6 8.9 collective-permute-start.11
  123.1 4.9 copy-start.2
  147.5 2.0 copy-start.1
  150.1 13.5 %copy-start = (f32[127,4,2,2048]{0,3,2,1:T(8,128)}, f32[127,4,2,2048]{0,3,2,1:T(8,128)S(1)}, u32[]{:S(2)}) copy-start(f32[127,4,2,2048]{0,3,2,1:T(8,128)S(1)} %pad_maximum_fusion) | copy-start | bytes 24969220
  752.5 30.1 %collective-permute-start.15 = (f32[4,2,2048]{2,1,0:T(2,128)S(1)}, f32[4,2,2048]{2,1,0:T(2,128)S(1)}, u32[]{:S(2)}, u32[]{:S(2)}) collective-permute-start(f32[4,2,2048]{2,1,0:T(2,128)S(1)} %fusion.86), channel_id=1, source_target_pairs={{1,0},{2,1},{3,2},{4,3},{5,4},{6,5},{7,6},{9,8},{10,9},{11,10},{12... | collective-permute-start | bytes 196616 | tf_op jit(solution)/shard_map/ppermute | solution.py:38
  785.9 5.0 collective-permute-start.16
  789.0 5.8 collective-permute-start.17
  794.9 4.7 collective-permute-start.18
  798.1 5.7 collective-permute-start.19
  803.9 14.7 %collective-permute-start.21 = (f32[5,2,2048]{2,1,0:T(2,128)S(1)}, f32[5,2,2048]{2,1,0:T(2,128)S(1)}, u32[]{:S(2)}, u32[]{:S(2)}) collective-permute-start(f32[5,2,2048]{2,1,0:T(2,128)S(1)} %pad_maximum_fusion.11), channel_id=1, source_target_pairs={{4,0},{5,1},{6,2},{7,3},{12,8},{13,9},{14,10},{15,11},{20,16},{21,... | collective-permute-start | bytes 245768 | tf_op jit(solution)/shard_map/ppermute | solution.py:38
  805.2 13.4 %collective-permute-start.20 = (f32[5,2,2048]{2,1,0:T(2,128)S(1)}, f32[5,2,2048]{2,1,0:T(2,128)S(1)}, u32[]{:S(2)}, u32[]{:S(2)}) collective-permute-start(f32[5,2,2048]{2,1,0:T(2,128)S(1)} %pad_maximum_fusion.11), channel_id=1, source_target_pairs={{0,4},{1,5},{2,6},{3,7},{8,12},{9,13},{10,14},{11,15},{16,20},{17,... | collective-permute-start | bytes 245768 | tf_op jit(solution)/shard_map/ppermute | solution.py:38
  810.7 12.1 %slice-start = ((s8[8126464]{0:T(1024)(128)(4,1)}), s8[4194304]{0:T(1024)(128)(4,1)S(1)}, s32[]{:S(2)}) async-start(s8[8126464]{0:T(1024)(128)(4,1)} %bitcast.462), calls=%async_computation.1 | async-start | bytes 8388608
  810.7 12.1 %slice-start.1 = ((s8[8126464]{0:T(1024)(128)(4,1)}), s8[3932160]{0:T(1024)(128)(4,1)S(1)}, s32[]{:S(2)}) async-start(s8[8126464]{0:T(1024)(128)(4,1)} %bitcast.462), calls=%async_computation.2 | async-start | bytes 7864320
  818.7 7.0 collective-permute-start.22
  850.4 4.9 copy-start.3
